TPU v7x, 32 devices: a whole 2x2x4 slice. The times are simulated.
32 devices in a mesh: row: 4 (over y, x), seq: 8 (over z, core).
Axes of the slice: x: 2, y: 2, z: 4, core: 2. Of those that a mesh axis runs over, the one named last changes fastest.
Arguments:
- hidden_in: bfloat16 [4, 1024, 1024], P('row', 'seq'), may hold values from -6 to 6
- segments: int32 [4, 1024], P('row', 'seq'), may hold values from 0 to 2, as said below
- routes: int32 [4, 1024, 8], P('row', 'seq'), may hold values from 0 to 15, all different within a row; in each aligned block of 128 rows (0 to 127, 128 to 255, ..., all dimensions but the last counted through in order) at most 80 rows name the same one
- cotangent: bfloat16 [4, 1024, 1024], P('row', 'seq'), may hold values from -6 to 6
- attn_gain: bfloat16 [1024], P(('row', 'seq')), may hold values from 0.5 to 1.5
- query_weight: bfloat16 [1024, 1024], P(('row', 'seq')), may hold values from -0.1875 to 0.1875
- key_weight: bfloat16 [1024, 512], P(('row', 'seq')), may hold values from -0.1875 to 0.1875
- value_weight: bfloat16 [1024, 512], P(('row', 'seq')), may hold values from -0.1875 to 0.1875
- out_weight: bfloat16 [1024, 1024], P(None, ('row', 'seq')), may hold values from -0.75 to 0.75
- ffn_gain: bfloat16 [1024], P(('row', 'seq')), may hold values from 0.5 to 1.5
- router_weight: bfloat16 [1024, 16], P(('row', 'seq')), may hold values from -0.09375 to 0.09375
- gate_weight: bfloat16 [16, 1024, 512], P('row', 'seq'), may hold values from -0.1875 to 0.1875
- up_weight: bfloat16 [16, 1024, 512], P('row', 'seq'), may hold values from -0.1875 to 0.1875
- down_weight: bfloat16 [16, 512, 1024], P('row', None, 'seq'), may hold values from -0.75 to 0.75
Outputs:
- hidden_out: bfloat16 [4, 1024, 1024], P('row', 'seq')
- hidden_grad: bfloat16 [4, 1024, 1024], P('row', 'seq')
- attn_gaingrad: float32 [1024], P(('row', 'seq'))
- query_grad: float32 [1024, 1024], P(('row', 'seq'))
- key_grad: float32 [1024, 512], P(('row', 'seq'))
- value_grad: float32 [1024, 512], P(('row', 'seq'))
- out_grad: float32 [1024, 1024], P(None, ('row', 'seq'))
- ffn_gaingrad: float32 [1024], P(('row', 'seq'))
- router_grad: float32 [1024, 16], P(('row', 'seq'))
- gate_grad: float32 [16, 1024, 512], P('row', 'seq')
- up_grad: float32 [16, 1024, 512], P('row', 'seq')
- down_grad: float32 [16, 512, 1024], P('row', None, 'seq')
Inputs may be any that keep to these rules, and one draw needn't show every extreme that they name: `segments`: in each row the ids never fall and run 0, 1, 2; segment 1 begins within the row's first 128 tokens but not at its first token, and ends within its last 128 tokens but before its last token. `routes`: the 8 experts of a token are all different. In each aligned block of 128 tokens of a packed row (that row's tokens on one device) no expert is named by more than 80 tokens, and in every draw some block has an expert named by exactly 80 tokens.
All inputs are finite; a program needn't handle non-finite values.
Results may differ from a plain program's by a relative error of at most 0.018.
Values may be sent and summed in bfloat16 or wider, within the bound.
No kernel may reach another device: no remote copies, remote signals or barrier semaphores. Data moves between devices by JAX's collectives and lax.ppermute only.
A program may use at most 256 MiB of HBM per device.

v0:
```python
import jax
import jax.numpy as jnp
from jax import lax
from jax.sharding import PartitionSpec as P

HEADS = 16
KV_HEADS = 8
HEAD_DIM = 64


EPS = 1e-06
THETA = 10000.0
NEG = -1e30


def rotate(values_in, cosine_part, sine_part):
    middle = values_in.shape[-1] // 2
    leading = values_in[..., :middle]
    trailing = values_in[..., middle:]
    return jnp.concatenate(
        [
            leading * cosine_part - trailing * sine_part,
            trailing * cosine_part + leading * sine_part,
        ],
        axis=-1,
    )


def slot_tables(routes, capacity, experts):
    block_total, block_len, choose = routes.shape
    onehot = (routes[..., None] == jnp.arange(experts, dtype=jnp.int32)).astype(jnp.int32)
    per_token = jnp.sum(onehot, axis=2)
    before = jnp.cumsum(per_token, axis=1) - per_token
    placed = jnp.take_along_axis(before, routes, axis=2)
    slot_ids = (routes * capacity + placed).reshape(block_total, block_len * choose)
    owners = jnp.repeat(jnp.arange(block_len, dtype=jnp.int32), choose)

    def fill_table(indices):
        return jnp.full((experts * capacity,), block_len, jnp.int32).at[indices].set(owners)

    return (slot_ids, jax.vmap(fill_table)(slot_ids))


def take_rows(source_rows, indices):

    def single(rows_here, pick_rows):
        return jnp.take(rows_here, pick_rows, axis=0)

    return jax.vmap(single)(source_rows, indices)


def shards(
    hidden_in,
    segments,
    routes,
    cotangent,
    attn_gain,
    query_weight,
    key_weight,
    value_weight,
    out_weight,
    ffn_gain,
    router_weight,
    gate_weight,
    up_weight,
    down_weight,
):
    seq_count = lax.axis_size("seq")
    seq_place = lax.axis_index("seq")
    row_count = lax.axis_size("row")
    seqs_here, block_len, model_width = hidden_in.shape
    choose = routes.shape[2]
    row_len = block_len * seq_count
    groups = HEADS // KV_HEADS
    middle = HEAD_DIM // 2
    score_scale = HEAD_DIM ** (-0.5)
    experts = router_weight.shape[1]
    capacity = block_len * 5 // 8
    key_block = min(512, row_len)
    key_steps = row_len // key_block
    kv_width = KV_HEADS * HEAD_DIM
    row_segments = lax.all_gather(segments, "seq", axis=1, tiled=True)
    gain_one, wq_full, wk_full, wv_full, wo_full, gain_two, router_full = (
        lax.all_gather(attn_gain, ("row", "seq"), axis=0, tiled=True),
        lax.all_gather(query_weight, ("row", "seq"), axis=0, tiled=True),
        lax.all_gather(key_weight, ("row", "seq"), axis=0, tiled=True),
        lax.all_gather(value_weight, ("row", "seq"), axis=0, tiled=True),
        lax.all_gather(out_weight, ("row", "seq"), axis=1, tiled=True),
        lax.all_gather(ffn_gain, ("row", "seq"), axis=0, tiled=True),
        lax.all_gather(router_weight, ("row", "seq"), axis=0, tiled=True),
    )
    local_gate, local_up, local_down = (
        lax.all_gather(gate_weight, "seq", axis=1, tiled=True),
        lax.all_gather(up_weight, "seq", axis=1, tiled=True),
        lax.all_gather(down_weight, "seq", axis=2, tiled=True),
    )
    query_index = seq_place * block_len + jnp.arange(block_len, dtype=jnp.int32)
    starts = jnp.sum((row_segments[:, None, :] < segments[:, :, None]).astype(jnp.int32), axis=2)
    positions = (query_index[None, :] - starts).astype(jnp.float32)
    frequency = THETA ** (-jnp.arange(middle, dtype=jnp.float32) * 2.0 / HEAD_DIM)
    angles = positions[..., None] * frequency
    cosines = jnp.cos(angles)
    sines = jnp.sin(angles)
    hidden_f = hidden_in.astype(jnp.float32)
    inv_one = lax.rsqrt(jnp.mean(hidden_f * hidden_f, axis=-1, keepdims=True) + EPS)
    attn_in = (hidden_f * inv_one * gain_one.astype(jnp.float32)).astype(jnp.bfloat16)
    query_pre = jnp.dot(attn_in, wq_full, preferred_element_type=jnp.float32)
    query_rot = rotate(
        query_pre.reshape(seqs_here, block_len, KV_HEADS, groups, HEAD_DIM),
        cosines[:, :, None, None],
        sines[:, :, None, None],
    ).astype(jnp.bfloat16)
    key_pre = jnp.dot(attn_in, wk_full, preferred_element_type=jnp.float32)
    key_rot = rotate(
        key_pre.reshape(seqs_here, block_len, KV_HEADS, HEAD_DIM),
        cosines[:, :, None],
        sines[:, :, None],
    ).astype(jnp.bfloat16)
    value_low = jnp.dot(attn_in, wv_full, preferred_element_type=jnp.float32).astype(jnp.bfloat16)
    key_all, value_all = (
        lax.all_gather(key_rot.reshape(seqs_here, block_len, kv_width), "seq", axis=1, tiled=True),
        lax.all_gather(value_low, "seq", axis=1, tiled=True),
    )
    key_all = key_all.reshape(seqs_here, row_len, KV_HEADS, HEAD_DIM)
    value_all = value_all.reshape(seqs_here, row_len, KV_HEADS, HEAD_DIM)

    def block_scores(step_num):
        offset = step_num * key_block
        keys_here = lax.dynamic_slice_in_dim(key_all, offset, key_block, 1)
        values_here = lax.dynamic_slice_in_dim(value_all, offset, key_block, 1)
        key_segs = lax.dynamic_slice_in_dim(row_segments, offset, key_block, 1)
        key_index = offset + jnp.arange(key_block, dtype=jnp.int32)
        scores = (
            jnp.einsum(
                "sckgd,sjkd->skgcj", query_rot, keys_here, preferred_element_type=jnp.float32
            )
            * score_scale
        )
        allowed = (key_index[None, None, :] <= query_index[None, :, None]) & (
            segments[:, :, None] == key_segs[:, None, :]
        )
        return (scores, allowed[:, None, None], keys_here, values_here)

    def stats_step(state_in, step_num):
        running, exp_total = state_in
        scores, allowed, keys_here, values_here = block_scores(step_num)
        masked = jnp.where(allowed, scores, NEG)
        updated = jnp.maximum(running, jnp.max(masked, axis=-1))
        exp_total = exp_total * jnp.exp(running - updated) + jnp.sum(
            jnp.where(allowed, jnp.exp(masked - updated[..., None]), 0.0), axis=-1
        )
        return ((updated, exp_total), None)

    stat_shape = (seqs_here, KV_HEADS, groups, block_len)
    (running, exp_total), unused = lax.scan(
        stats_step,
        (jnp.full(stat_shape, NEG, jnp.float32), jnp.zeros(stat_shape, jnp.float32)),
        jnp.arange(key_steps),
    )
    log_total = running + jnp.log(exp_total)

    def mix_step(accumulated, step_num):
        scores, allowed, keys_here, values_here = block_scores(step_num)
        probability = jnp.where(allowed, jnp.exp(scores - log_total[..., None]), 0.0).astype(
            jnp.bfloat16
        )
        return (
            accumulated
            + jnp.einsum(
                "skgcj,sjkd->sckgd", probability, values_here, preferred_element_type=jnp.float32
            ),
            None,
        )

    mix_full, unused = lax.scan(
        mix_step,
        jnp.zeros((seqs_here, block_len, KV_HEADS, groups, HEAD_DIM), jnp.float32),
        jnp.arange(key_steps),
    )
    mix_low = mix_full.reshape(seqs_here, block_len, HEADS * HEAD_DIM).astype(jnp.bfloat16)
    residual = hidden_f + jnp.dot(mix_low, wo_full, preferred_element_type=jnp.float32)
    inv_two = lax.rsqrt(jnp.mean(residual * residual, axis=-1, keepdims=True) + EPS)
    ffn_in = (residual * inv_two * gain_two.astype(jnp.float32)).astype(jnp.bfloat16)
    logits = jnp.dot(ffn_in, router_full, preferred_element_type=jnp.float32)
    gate_probs = jax.nn.softmax(jnp.take_along_axis(logits, routes, axis=2), axis=-1)
    slot_ids, token_of = slot_tables(routes, capacity, experts)
    padded = jnp.concatenate([ffn_in, jnp.zeros((seqs_here, 1, model_width), jnp.bfloat16)], axis=1)
    buffer = take_rows(padded, token_of).reshape(seqs_here, experts, capacity, model_width)
    gate_full, up_full, down_full = (local_gate, local_up, local_down)
    work_rows = lax.all_to_all(buffer, "row", split_axis=1, concat_axis=1, tiled=True)
    work_shape = (seqs_here, row_count, experts // row_count, capacity, model_width)
    work_rows = work_rows.reshape(work_shape)
    gate_pre = jnp.einsum(
        "srecd,edf->srecf", work_rows, gate_full, preferred_element_type=jnp.float32
    )
    up_pre = jnp.einsum("srecd,edf->srecf", work_rows, up_full, preferred_element_type=jnp.float32)
    hidden_act = (jax.nn.silu(gate_pre) * up_pre).astype(jnp.bfloat16)
    expert_out = (
        jnp.einsum("srecf,efd->srecd", hidden_act, down_full, preferred_element_type=jnp.float32)
        .astype(jnp.bfloat16)
        .reshape(seqs_here, experts, capacity, model_width)
    )
    expert_out = lax.all_to_all(expert_out, "row", split_axis=1, concat_axis=1, tiled=True)
    routed = (
        take_rows(expert_out.reshape(seqs_here, experts * capacity, model_width), slot_ids)
        .reshape(seqs_here, block_len, choose, model_width)
        .astype(jnp.float32)
    )
    hidden_out = (residual + jnp.sum(gate_probs[..., None] * routed, axis=2)).astype(jnp.bfloat16)
    upstream = cotangent.astype(jnp.float32)
    gate_slope = jnp.sum(upstream[:, :, None, :] * routed, axis=-1)
    routed_slope = (
        (gate_probs[..., None] * upstream[:, :, None, :])
        .astype(jnp.bfloat16)
        .reshape(seqs_here, block_len * choose, model_width)
    )

    def place_rows(slope_rows, indices):
        return (
            jnp.zeros((experts * capacity, model_width), jnp.bfloat16).at[indices].set(slope_rows)
        )

    expert_slope = jax.vmap(place_rows)(routed_slope, slot_ids).reshape(
        seqs_here, experts, capacity, model_width
    )
    expert_slope = lax.all_to_all(expert_slope, "row", split_axis=1, concat_axis=1, tiled=True)
    slope_rows = expert_slope.reshape(work_shape)
    gate_pre = jnp.einsum(
        "srecd,edf->srecf", work_rows, gate_full, preferred_element_type=jnp.float32
    )
    up_pre = jnp.einsum("srecd,edf->srecf", work_rows, up_full, preferred_element_type=jnp.float32)
    hidden_act = (jax.nn.silu(gate_pre) * up_pre).astype(jnp.bfloat16)
    hidden_slope = jnp.einsum(
        "srecd,efd->srecf", slope_rows, down_full, preferred_element_type=jnp.float32
    )
    down_part = jnp.einsum(
        "srecf,srecd->efd", hidden_act, slope_rows, preferred_element_type=jnp.float32
    )
    sigmoid_gate = jax.nn.sigmoid(gate_pre)
    gate_low = (
        hidden_slope * up_pre * sigmoid_gate * (1.0 + gate_pre * (1.0 - sigmoid_gate))
    ).astype(jnp.bfloat16)
    up_low = (hidden_slope * gate_pre * sigmoid_gate).astype(jnp.bfloat16)
    gate_part = jnp.einsum(
        "srecd,srecf->edf", work_rows, gate_low, preferred_element_type=jnp.float32
    )
    up_part = jnp.einsum("srecd,srecf->edf", work_rows, up_low, preferred_element_type=jnp.float32)
    buffer_slope = (
        (
            jnp.einsum("srecf,edf->srecd", gate_low, gate_full, preferred_element_type=jnp.float32)
            + jnp.einsum("srecf,edf->srecd", up_low, up_full, preferred_element_type=jnp.float32)
        )
        .astype(jnp.bfloat16)
        .reshape(seqs_here, experts, capacity, model_width)
    )
    buffer_slope = lax.all_to_all(buffer_slope, "row", split_axis=1, concat_axis=1, tiled=True)
    group_parts = (gate_part, up_part, down_part)
    expert_shares = (
        lax.psum_scatter(
            group_parts[0].astype(jnp.bfloat16), "seq", scatter_dimension=1, tiled=True
        ).astype(jnp.float32),
        lax.psum_scatter(
            group_parts[1].astype(jnp.bfloat16), "seq", scatter_dimension=1, tiled=True
        ).astype(jnp.float32),
        lax.psum_scatter(
            group_parts[2].astype(jnp.bfloat16), "seq", scatter_dimension=2, tiled=True
        ).astype(jnp.float32),
    )
    token_slope = jnp.sum(
        take_rows(buffer_slope.reshape(seqs_here, experts * capacity, model_width), slot_ids)
        .reshape(seqs_here, block_len, choose, model_width)
        .astype(jnp.float32),
        axis=2,
    )
    chosen_slope = gate_probs * (
        gate_slope - jnp.sum(gate_probs * gate_slope, axis=-1, keepdims=True)
    )
    onehot = routes[..., None] == jnp.arange(experts, dtype=jnp.int32)
    logit_slope = jnp.sum(jnp.where(onehot, chosen_slope[..., None], 0.0), axis=2).astype(
        jnp.bfloat16
    )
    router_grad = jnp.einsum("scd,sce->de", ffn_in, logit_slope, preferred_element_type=jnp.float32)
    ffn_slope = token_slope + jnp.dot(
        logit_slope, router_full.T, preferred_element_type=jnp.float32
    )
    scaled_two = ffn_slope * gain_two.astype(jnp.float32)
    ffn_gaingrad = jnp.sum(ffn_slope * residual * inv_two, axis=(0, 1))
    resid_slope = (
        upstream
        + inv_two * scaled_two
        - residual * inv_two**3 * jnp.mean(scaled_two * residual, axis=-1, keepdims=True)
    )
    branch_low = resid_slope.astype(jnp.bfloat16)
    out_grad = jnp.einsum("sch,scd->hd", mix_low, branch_low, preferred_element_type=jnp.float32)
    mix_slope = (
        jnp.dot(branch_low, wo_full.T, preferred_element_type=jnp.float32)
        .astype(jnp.bfloat16)
        .reshape(seqs_here, block_len, KV_HEADS, groups, HEAD_DIM)
    )
    row_delta = jnp.sum(mix_slope.astype(jnp.float32) * mix_full, axis=-1).transpose(0, 2, 3, 1)

    def slope_step(state_in, step_num):
        query_acc, key_acc, value_acc = state_in
        scores, allowed, keys_here, values_here = block_scores(step_num)
        probability = jnp.where(allowed, jnp.exp(scores - log_total[..., None]), 0.0)
        value_part = jnp.einsum(
            "skgcj,sckgd->sjkd",
            probability.astype(jnp.bfloat16),
            mix_slope,
            preferred_element_type=jnp.float32,
        )
        prob_slope = jnp.einsum(
            "sckgd,sjkd->skgcj", mix_slope, values_here, preferred_element_type=jnp.float32
        )
        score_low = (probability * (prob_slope - row_delta[..., None])).astype(jnp.bfloat16)
        query_acc = query_acc + score_scale * jnp.einsum(
            "skgcj,sjkd->sckgd", score_low, keys_here, preferred_element_type=jnp.float32
        )
        key_part = score_scale * jnp.einsum(
            "skgcj,sckgd->sjkd", score_low, query_rot, preferred_element_type=jnp.float32
        )
        offset = step_num * key_block
        key_acc = lax.dynamic_update_slice_in_dim(
            key_acc, key_part.reshape(seqs_here, key_block, kv_width), offset, 1
        )
        value_acc = lax.dynamic_update_slice_in_dim(
            value_acc, value_part.reshape(seqs_here, key_block, kv_width), offset, 1
        )
        return ((query_acc, key_acc, value_acc), None)

    slope_init = (
        jnp.zeros((seqs_here, block_len, KV_HEADS, groups, HEAD_DIM), jnp.float32),
        jnp.zeros((seqs_here, row_len, kv_width), jnp.float32),
        jnp.zeros((seqs_here, row_len, kv_width), jnp.float32),
    )
    (query_acc, key_acc, value_acc), unused = lax.scan(
        slope_step, slope_init, jnp.arange(key_steps)
    )
    key_share, value_share = (
        lax.psum_scatter(
            key_acc.astype(jnp.bfloat16), "seq", scatter_dimension=1, tiled=True
        ).astype(jnp.float32),
        lax.psum_scatter(
            value_acc.astype(jnp.bfloat16), "seq", scatter_dimension=1, tiled=True
        ).astype(jnp.float32),
    )
    query_low = (
        rotate(query_acc, cosines[:, :, None, None], -sines[:, :, None, None])
        .reshape(seqs_here, block_len, HEADS * HEAD_DIM)
        .astype(jnp.bfloat16)
    )
    key_low = (
        rotate(
            key_share.reshape(seqs_here, block_len, KV_HEADS, HEAD_DIM),
            cosines[:, :, None],
            -sines[:, :, None],
        )
        .reshape(seqs_here, block_len, kv_width)
        .astype(jnp.bfloat16)
    )
    value_slope = value_share.astype(jnp.bfloat16)
    query_grad = jnp.einsum("scd,sch->dh", attn_in, query_low, preferred_element_type=jnp.float32)
    key_grad = jnp.einsum("scd,sch->dh", attn_in, key_low, preferred_element_type=jnp.float32)
    value_grad = jnp.einsum("scd,sch->dh", attn_in, value_slope, preferred_element_type=jnp.float32)
    attn_slope = (
        jnp.dot(query_low, wq_full.T, preferred_element_type=jnp.float32)
        + jnp.dot(key_low, wk_full.T, preferred_element_type=jnp.float32)
        + jnp.dot(value_slope, wv_full.T, preferred_element_type=jnp.float32)
    )
    scaled_one = attn_slope * gain_one.astype(jnp.float32)
    attn_gaingrad = jnp.sum(attn_slope * hidden_f * inv_one, axis=(0, 1))
    input_slope = (
        resid_slope
        + inv_one * scaled_one
        - hidden_f * inv_one**3 * jnp.mean(scaled_one * hidden_f, axis=-1, keepdims=True)
    )
    hidden_grad = input_slope.astype(jnp.bfloat16)
    dense_shares = (
        lax.psum_scatter(attn_gaingrad, ("row", "seq"), scatter_dimension=0, tiled=True),
        lax.psum_scatter(query_grad, ("row", "seq"), scatter_dimension=0, tiled=True),
        lax.psum_scatter(key_grad, ("row", "seq"), scatter_dimension=0, tiled=True),
        lax.psum_scatter(value_grad, ("row", "seq"), scatter_dimension=0, tiled=True),
        lax.psum_scatter(out_grad, ("row", "seq"), scatter_dimension=1, tiled=True),
        lax.psum_scatter(ffn_gaingrad, ("row", "seq"), scatter_dimension=0, tiled=True),
        lax.psum_scatter(router_grad, ("row", "seq"), scatter_dimension=0, tiled=True),
    )
    return (
        hidden_out,
        hidden_grad,
        dense_shares[0],
        dense_shares[1],
        dense_shares[2],
        dense_shares[3],
        dense_shares[4],
        dense_shares[5],
        dense_shares[6],
        expert_shares[0],
        expert_shares[1],
        expert_shares[2],
    )


def solution(mesh):
    return jax.shard_map(
        shards,
        mesh=mesh,
        in_specs=(
            P("row", "seq", None),
            P("row", "seq"),
            P("row", "seq", None),
            P("row", "seq", None),
            P(("row", "seq")),
            P(("row", "seq"), None),
            P(("row", "seq"), None),
            P(("row", "seq"), None),
            P(None, ("row", "seq")),
            P(("row", "seq")),
            P(("row", "seq"), None),
            P("row", "seq", None),
            P("row", "seq", None),
            P("row", None, "seq"),
        ),
        out_specs=(
            P("row", "seq", None),
            P("row", "seq", None),
            P(("row", "seq")),
            P(("row", "seq"), None),
            P(("row", "seq"), None),
            P(("row", "seq"), None),
            P(None, ("row", "seq")),
            P(("row", "seq")),
            P(("row", "seq"), None),
            P("row", "seq", None),
            P("row", "seq", None),
            P("row", None, "seq"),
        ),
        check_vma=False,
    )
```

profile of v0, /device:TPU:0, one launch (start us, length us, event | category | flops | bytes accessed | tf_op | source)
XLA Modules:
  0.0 1569.6 jit_solution(17931830671620670408)
XLA Ops:
  10.4 42.0 %all-reduce.6 = (bf16[1024]{0:T(1024)(128)(2,1)S(1)}, bf16[1024]{0:T(1024)(128)(2,1)S(1)}) all-reduce(bf16[1024]{0:T(1024)(128)(2,1)S(1)} %dynamic-update-slice, bf16[1024]{0:T(1024)(128)(2,1)S(1)} %dynamic-update-slice.1), channel_id=1, replica_groups=mesh['row'=4,'seq'=8] {'row','seq'}, use_global_device_ids=true, to_apply=%add.1 | all-reduce | flops 2048 | bytes 8192
  83.0 40.4 %all-gather.14.cloned.1.call-done = bf16[1024,512]{1,0:T(8,128)(2,1)} async-done(((bf16[32,512]{1,0:T(8,128)(2,1)}), bf16[1024,512]{1,0:T(8,128)(2,1)}) %all-gather.14.cloned.1.call-update) | async-done | bytes 1048592 | tf_op jit(solution)/shard_map/all_gather | solution.py:86
  148.9 56.7 %all-gather.18.cloned.1.call-done = bf16[1024,1024]{1,0:T(8,128)(2,1)} async-done(((bf16[32,1024]{1,0:T(8,128)(2,1)}), bf16[1024,1024]{1,0:T(8,128)(2,1)}) %all-gather.18.cloned.1.call-update) | async-done | bytes 2097168 | tf_op jit(solution)/shard_map/all_gather | solution.py:85
  209.4 21.1 %all-gather.16.cloned.1.call-done = bf16[1,1024,512]{1,2,0:T(8,128)(2,1)} async-done(((bf16[1,128,512]{1,2,0:T(8,128)(2,1)}), bf16[1,1024,512]{1,2,0:T(8,128)(2,1)}) %all-gather.16.cloned.1.call-update) | async-done | bytes 1048592 | tf_op jit(solution)/shard_map/all_gather | solution.py:121
  230.5 17.1 %while.39 = (s32[]{:T(128)}, f32[1,8,2,128]{3,2,1,0:T(2,128)S(1)}, f32[1,8,2,128]{3,2,1,0:T(2,128)S(1)}, s32[2]{0:T(128)S(1)}, s32[1,128]{1,0:T(1,128)S(1)}, /*i...) while((s32[]{:T(128)}, f32[1,8,2,128]{3,2,1,0:T(2,128)S(1)}, ...), condition=%wide.region_5.6_spmd.clone, body=%wide.region_2.5_spmd.clone.sunk | while | flops 142813824 | bytes 9490138 | solution.py:155
  255.5 32.9 %all-gather.20.cloned.1.call-done = bf16[1024,1024]{0,1:T(8,128)(2,1)} async-done(((bf16[1024,32]{0,1:T(8,128)(2,1)}), bf16[1024,1024]{0,1:T(8,128)(2,1)}) %all-gather.20.cloned.1.call-update) | async-done | bytes 2097168 | tf_op jit(solution)/shard_map/all_gather | solution.py:88
  303.7 34.4 %all_to_all.20 = bf16[1,16,80,1024]{3,2,0,1:T(8,128)(2,1)S(1)} all-to-all(bf16[1,16,80,1024]{3,2,0,1:T(8,128)(2,1)S(1)} %broadcast_select_fusion.1), channel_id=1, replica_groups=mesh['row'=4,'seq'=8] {'row'}, dimensions={1} | all-to-all | bytes 5242880 | tf_op jit(solution)/shard_map/all_to_all | solution.py:190
  344.2 39.3 %all-gather.24.cloned.1.call-done = bf16[4,1024,512]{2,1,0:T(8,128)(2,1)} async-done(((bf16[4,128,512]{2,1,0:T(8,128)(2,1)}), bf16[4,1024,512]{2,1,0:T(8,128)(2,1)}) %all-gather.24.cloned.1.call-update) | async-done | bytes 4194320 | tf_op jit(solution)/shard_map/all_gather | solution.py:94
  390.2 41.5 %all-gather.26.cloned.1.call-done = bf16[4,512,1024]{2,1,0:T(8,128)(2,1)} async-done(((bf16[4,512,128]{2,1,0:T(8,128)(2,1)}), bf16[4,512,1024]{2,1,0:T(8,128)(2,1)}) %all-gather.26.cloned.1.call-update) | async-done | bytes 4194320 | tf_op jit(solution)/shard_map/all_gather | solution.py:95
  441.6 40.6 %all-gather.1 = bf16[32,32,16]{1,2,0:T(8,128)(2,1)S(1)} all-gather(bf16[1,32,16]{1,2,0:T(8,128)(2,1)S(1)} %bitcast.647), channel_id=1, replica_groups=mesh['row'=4,'seq'=8] {'row','seq'}, dimensions={0}, use_global_device_ids=true | all-gather | bytes 33792 | tf_op jit(solution)/shard_map/all_gather | solution.py:90
  493.1 14.1 gather_fusion.3
  516.9 34.9 %all_to_all.21 = bf16[1,16,80,1024]{3,2,0,1:T(8,128)(2,1)S(1)} all-to-all(bf16[1,16,80,1024]{3,2,0,1:T(8,128)(2,1)S(1)} %bitcast.604), channel_id=1, replica_groups=mesh['row'=4,'seq'=8] {'row'}, dimensions={1} | all-to-all | bytes 5242880 | tf_op jit(solution)/shard_map/all_to_all | solution.py:226
  572.1 25.8 %all-to-all-done.3 = bf16[1,16,80,1024]{3,2,0,1:T(8,128)(2,1)S(1)} async-done(((bf16[1,16,80,1024]{3,2,0,1:T(8,128)(2,1)}), bf16[1,16,80,1024]{3,2,0,1:T(8,128)(2,1)S(1)}, u32[]{:S(2)}, u32[]{:S(2)}) %all-to-all-start.3) | async-done | bytes 2621472 | tf_op jit(solution)/shard_map/all_to_all | solution.py:256
  597.9 14.1 gather_fusion.4
  622.0 27.5 %while.41 = (s32[]{:T(128)}, f32[1,128,8,2,64]{1,4,3,2,0:T(8,128)S(1)}, bf16[1,1024,512]{1,2,0:T(8,128)(2,1)}, bf16[1,1024,512]{1,2,0:T(8,128)(2,1)}, s32[2]{0:T...) while((s32[]{:T(128)}, ...), condition=%wide.region_23.25_spmd.clone, body=%wide.region_22.24_spmd.clone.sunk | while | flops 682689152 | bytes 63672244 | solution.py:336
  701.2 17.2 %reduce-scatter.33.cloned.1.call-done = bf16[128,512]{1,0:T(8,128)(2,1)} async-done(((bf16[1024,512]{1,0:T(8,128)(2,1)}), bf16[128,512]{1,0:T(8,128)(2,1)}) %reduce-scatter.33.cloned.1.call-update) | async-done | bytes 131088
  728.4 125.2 %reduce-scatter.35.cloned.1.call-done = f32[32,16]{1,0:T(8,128)} async-done(((f32[1024,16]{1,0:T(8,128)}), f32[32,16]{1,0:T(8,128)}) %reduce-scatter.35.cloned.1.call-update) | async-done | bytes 2064
  857.3 38.7 %all-reduce.5 = (f32[1024]{0:T(1024)S(1)}, f32[1024]{0:T(1024)S(1)}) all-reduce(f32[1024]{0:T(1024)S(1)} %get-tuple-element.336, f32[1024]{0:T(1024)S(1)} %get-tuple-element.334), channel_id=5, replica_groups=mesh['row'=4,'seq'=8] {'row','seq'}, use_global_device_ids=true, to_apply=%region_28.30.clone | all-reduce | flops 2048 | bytes 16384
  906.2 47.6 %reduce-scatter.27.cloned.1.call-done = bf16[4,128,512]{2,1,0:T(8,128)(2,1)} async-done(((bf16[4,1024,512]{2,1,0:T(8,128)(2,1)}), bf16[4,128,512]{2,1,0:T(8,128)(2,1)}) %reduce-scatter.27.cloned.1.call-update) | async-done | bytes 524304 | tf_op jit(solution)/shard_map/reduce_scatter | solution.py:259
  955.9 48.3 %reduce-scatter.29.cloned.1.call-done = bf16[4,128,512]{2,1,0:T(8,128)(2,1)} async-done(((bf16[4,1024,512]{2,1,0:T(8,128)(2,1)}), bf16[4,128,512]{2,1,0:T(8,128)(2,1)}) %reduce-scatter.29.cloned.1.call-update) | async-done | bytes 524304 | tf_op jit(solution)/shard_map/reduce_scatter | solution.py:262
  1006.4 135.9 %reduce-scatter.21.cloned.1.call-done = f32[32,512]{1,0:T(8,128)} async-done(((f32[1024,512]{1,0:T(8,128)}), f32[32,512]{1,0:T(8,128)}) %reduce-scatter.21.cloned.1.call-update) | async-done | bytes 65552 | tf_op jit(solution)/shard_map/reduce_scatter | solution.py:381
  1142.3 135.5 %reduce-scatter.23.cloned.1.call-done = f32[32,512]{1,0:T(8,128)} async-done(((f32[1024,512]{1,0:T(8,128)}), f32[32,512]{1,0:T(8,128)}) %reduce-scatter.23.cloned.1.call-update) | async-done | bytes 65552 | tf_op jit(solution)/shard_map/reduce_scatter | solution.py:382
  1277.8 142.7 %reduce-scatter.19.cloned.1.call-done = f32[32,1024]{1,0:T(8,128)} async-done(((f32[1024,1024]{1,0:T(8,128)}), f32[32,1024]{1,0:T(8,128)}) %reduce-scatter.19.cloned.1.call-update) | async-done | bytes 131088 | tf_op jit(solution)/shard_map/reduce_scatter | solution.py:380
  1420.4 142.4 %reduce-scatter.25.cloned.1.call-done = f32[1024,32]{0,1:T(8,128)} async-done(((f32[1024,1024]{0,1:T(8,128)}), f32[1024,32]{0,1:T(8,128)}) %reduce-scatter.25.cloned.1.call-update) | async-done | bytes 131088 | tf_op jit(solution)/shard_map/reduce_scatter | solution.py:383
  (378 shorter events, 286.6 us)
Async XLA Ops:
  7.2 60.4 %all-gather.12.cloned.1.call-start = ((), (), s32[]{:S(2)}) async-start(), calls=%async_computation.14 | async-start | bytes 1081344 | tf_op jit(solution)/shard_map/all_gather | solution.py:87
  7.9 115.4 %all-gather.14.cloned.1.call-start = ((), (), s32[]{:S(2)}) async-start(), calls=%async_computation.15 | async-start | bytes 1081344 | tf_op jit(solution)/shard_map/all_gather | solution.py:86
  8.7 138.0 %all-gather.28.cloned.1.call-start = ((), (), s32[]{:S(2)}) async-start(), calls=%async_computation.28 | async-start | bytes 1179648 | tf_op jit(solution)/shard_map/all_gather | solution.py:122
  52.5 156.0 %copy-start.38 = (f32[1024]{0:T(1024)}, f32[1024]{0:T(1024)S(1)}, u32[]{:S(2)}) copy-start(f32[1024]{0:T(1024)S(1)} %convert_element_type.292) | copy-start | bytes 12292
  54.1 154.4 %copy-start.49 = (f32[128]{0:T(128)}, f32[128]{0:T(128)S(1)}, u32[]{:S(2)}) copy-start(f32[128]{0:T(128)S(1)} %get-tuple-element.432) | copy-start | bytes 1540
  69.9 135.7 %all-gather.18.cloned.1.call-start = ((), (), s32[]{:S(2)}) async-start(), calls=%async_computation.17 | async-start | bytes 2162688 | tf_op jit(solution)/shard_map/all_gather | solution.py:85
  70.5 160.0 %all-gather.16.cloned.1.call-start = ((), (), s32[]{:S(2)}) async-start(), calls=%async_computation.16 | async-start | bytes 1179648 | tf_op jit(solution)/shard_map/all_gather | solution.py:121
  126.1 162.3 %all-gather.20.cloned.1.call-start = ((), (), s32[]{:S(2)}) async-start(), calls=%async_computation.18 | async-start | bytes 2162688 | tf_op jit(solution)/shard_map/all_gather | solution.py:88
  126.7 211.4 %all-gather.22.cloned.1.call-start = ((), (), s32[]{:S(2)}) async-start(), calls=%async_computation.19 | async-start | bytes 4718592 | tf_op jit(solution)/shard_map/all_gather | solution.py:93
  127.5 256.1 %all-gather.24.cloned.1.call-start = ((), (), s32[]{:S(2)}) async-start(), calls=%async_computation.20 | async-start | bytes 4718592 | tf_op jit(solution)/shard_map/all_gather | solution.py:94
  128.2 303.5 %all-gather.26.cloned.1.call-start = ((), (), s32[]{:S(2)}) async-start(), calls=%async_computation.21 | async-start | bytes 4718592 | tf_op jit(solution)/shard_map/all_gather | solution.py:95
  142.8 148.7 %copy-start.45 = (f32[1024]{0:T(1024)}, f32[1024]{0:T(1024)S(1)}, u32[]{:S(2)}) copy-start(f32[1024]{0:T(1024)S(1)} %convert_element_type.301) | copy-start | bytes 12292
  437.7 55.4 %all-to-all-start.1 = ((bf16[1,16,80,1024]{3,2,0,1:T(8,128)(2,1)}), bf16[1,16,80,1024]{3,2,0,1:T(8,128)(2,1)S(1)}, u32[]{:S(2)}, u32[]{:S(2)}) async-start(bf16[1,16,80,1024]{3,2,0,1:T(8,128)(2,1)} %bitcast.602), calls=%async_computation.1 | async-start | bytes 5242880 | tf_op jit(solution)/shard_map/all_to_all | solution.py:203
  564.2 33.7 %all-to-all-start.3 = ((bf16[1,16,80,1024]{3,2,0,1:T(8,128)(2,1)}), bf16[1,16,80,1024]{3,2,0,1:T(8,128)(2,1)S(1)}, u32[]{:S(2)}, u32[]{:S(2)}) async-start(bf16[1,16,80,1024]{3,2,0,1:T(8,128)(2,1)} %bitcast.603), calls=%async_computation.3 | async-start | bytes 5242880 | tf_op jit(solution)/shard_map/all_to_all | solution.py:256
  568.0 129.8 %reduce-scatter.31.cloned.1.call-start = ((), (), s32[]{:S(2)}) async-start(), calls=%async_computation.29 | async-start | bytes 1179648
  655.5 63.0 %reduce-scatter.33.cloned.1.call-start = ((), (), s32[]{:S(2)}) async-start(), calls=%async_computation.30 | async-start | bytes 1179648
  661.4 192.1 %reduce-scatter.35.cloned.1.call-start = ((), (), s32[]{:S(2)}) async-start(), calls=%async_computation.31 | async-start | bytes 540672
  662.6 240.8 %reduce-scatter.37.cloned.1.call-start = ((), (), s32[]{:S(2)}) async-start(), calls=%async_computation.32 | async-start | bytes 4718592
  682.8 271.0 %reduce-scatter.27.cloned.1.call-start = ((), (), s32[]{:S(2)}) async-start(), calls=%async_computation.26 | async-start | bytes 4718592 | tf_op jit(solution)/shard_map/reduce_scatter | solution.py:259
  690.3 313.9 %reduce-scatter.29.cloned.1.call-start = ((), (), s32[]{:S(2)}) async-start(), calls=%async_computation.27 | async-start | bytes 4718592 | tf_op jit(solution)/shard_map/reduce_scatter | solution.py:262
  697.8 444.5 %reduce-scatter.21.cloned.1.call-start = ((), (), s32[]{:S(2)}) async-start(), calls=%async_computation.23 | async-start | bytes 2162688 | tf_op jit(solution)/shard_map/reduce_scatter | solution.py:381
  701.2 576.6 %reduce-scatter.23.cloned.1.call-start = ((), (), s32[]{:S(2)}) async-start(), calls=%async_computation.24 | async-start | bytes 2162688 | tf_op jit(solution)/shard_map/reduce_scatter | solution.py:382
  721.6 698.8 %reduce-scatter.19.cloned.1.call-start = ((), (), s32[]{:S(2)}) async-start(), calls=%async_computation.22 | async-start | bytes 4325376 | tf_op jit(solution)/shard_map/reduce_scatter | solution.py:380
  724.5 838.3 %reduce-scatter.25.cloned.1.call-start = ((), (), s32[]{:S(2)}) async-start(), calls=%async_computation.25 | async-start | bytes 4325376 | tf_op jit(solution)/shard_map/reduce_scatter | solution.py:383
  (65 other events, 904.7 us)
Sparse Core Ops, SparseCore 0:
  11.0 56.4 all-gather.11
  70.5 52.7 all-gather.13
  125.5 21.0 all-gather.27
  149.5 56.0 all-gather.17
  207.6 22.8 all-gather.15
  233.3 55.0 all-gather.19
  290.0 45.9 all-gather.21
  337.7 45.8 all-gather.23
  385.1 46.5 all-gather.25
  655.6 29.5 reduce-scatter.30
  688.0 30.3 reduce-scatter.32
  721.1 132.4 reduce-scatter.34
  856.0 47.3 reduce-scatter.36
  905.6 48.1 reduce-scatter.26
  956.0 48.1 reduce-scatter.28
  1007.0 135.2 reduce-scatter.20
  1145.0 132.7 reduce-scatter.22
  1280.6 139.8 reduce-scatter.18
  1423.4 139.3 reduce-scatter.24
where the time goes:
time: 1580 us; the launch traced here: 1570 us
  waiting for transfers between devices  1080 us (68%)
  blocking collectives  201 us (13%)
  local copies, waits for them, and re-layouts  123 us (8%)
  matrix products  97.2 us (6%)
  other arithmetic  40.6 us (3%)
    unnamed x23, waiting for transfers between devices  152 us
    reduce_scatter x1, waiting for transfers between devices, shards(): lax.psum_scatter(query_grad, ('row', 'seq'), scatter_dimension=0, tiled=T...  143 us
    reduce_scatter x1, waiting for transfers between devices, shards(): lax.psum_scatter(out_grad, ('row', 'seq'), scatter_dimension=1, tiled=True)  142 us
    reduce_scatter x1, waiting for transfers between devices, shards(): lax.psum_scatter(key_grad, ('row', 'seq'), scatter_dimension=0, tiled=True)  136 us
    reduce_scatter x1, waiting for transfers between devices, shards(): lax.psum_scatter(value_grad, ('row', 'seq'), scatter_dimension=0, tiled=T...  135 us
    unnamed x2, blocking collectives  80.8 us
    all_gather x1, waiting for transfers between devices, shards(): lax.all_gather(query_weight, ('row', 'seq'), axis=0, tiled=True)  56.7 us
    reduce_scatter x1, waiting for transfers between devices, shards(): lax.psum_scatter(group_parts[1].astype(jnp.bfloat16), 'seq', scatter_dime...  48.3 us
  transfers between devices with their start and end apart: 21, of which 18 were waited for; matrix products, arithmetic and copies ran while one was open for 10% of the time, Pallas kernels for 0%

commit v1 on v0

v1 whole, which is shorter than its diff:
```python
import jax
import jax.numpy as jnp
from jax import lax
from jax.sharding import Mesh
from jax.sharding import PartitionSpec as P

HEADS = 16
KV_HEADS = 8
HEAD_DIM = 64

EPS = 1e-06
THETA = 10000.0
NEG = -1e30
GROUP = 4

BF = jnp.bfloat16
F32 = jnp.float32

SEQ = ("zh", "zl", "core")
DEPTH = ("zh", "zl")
ALL = ("row", "zh", "zl", "core")
TEAM = ("row", "zl")


def nt(left, right):
    return lax.dot_general(left, right, (((1,), (1,)), ((), ())), preferred_element_type=F32)


def nn(left, right):
    return lax.dot_general(left, right, (((1,), (0,)), ((), ())), preferred_element_type=F32)


def tn(left, right):
    return lax.dot_general(left, right, (((0,), (0,)), ((), ())), preferred_element_type=F32)


def pad_to(flat, size):
    return jnp.concatenate([flat, jnp.zeros((size - flat.shape[0],), flat.dtype)])


def rotate(values_in, cosines, sines):
    tokens, width = values_in.shape
    heads = values_in.reshape(tokens, width // HEAD_DIM, 2, HEAD_DIM // 2)
    first, second = heads[:, :, 0], heads[:, :, 1]
    cosines, sines = cosines[:, None], sines[:, None]
    turned = jnp.stack([first * cosines - second * sines, second * cosines + first * sines], axis=2)
    return turned.reshape(tokens, width)


def shards(
    hidden_in,
    segments,
    routes,
    cotangent,
    attn_gain,
    query_weight,
    key_weight,
    value_weight,
    out_weight,
    ffn_gain,
    router_weight,
    gate_weight,
    up_weight,
    down_weight,
):
    rows = lax.axis_size("row")
    far, near, cores = lax.axis_size("zh"), lax.axis_size("zl"), lax.axis_size("core")
    depth = far * near
    seqs = depth * cores
    span, width = hidden_in.shape[1:]
    length = span * seqs
    feats = query_weight.shape[0]
    experts = router_weight.shape[1]
    held, slab, hidden = gate_weight.shape
    mine = held // near
    heads = HEADS // seqs
    groups = HEADS // KV_HEADS
    key_heads = max(1, heads // groups)
    query_cols, key_cols = heads * HEAD_DIM, key_heads * HEAD_DIM
    cols = query_cols + 2 * key_cols
    scale = HEAD_DIM**-0.5

    own = hidden_in[0]
    row_hidden = lax.all_gather(own, SEQ, axis=0, tiled=True)

    def key_start(place):
        return (place * heads // groups) * HEAD_DIM

    query_part = query_weight.reshape(feats, seqs, query_cols)
    key_part = jnp.stack([key_weight[:, key_start(s) : key_start(s) + key_cols] for s in range(seqs)], 1)
    value_part = jnp.stack([value_weight[:, key_start(s) : key_start(s) + key_cols] for s in range(seqs)], 1)
    dense = jnp.concatenate([query_part, key_part, value_part], axis=2).transpose(1, 0, 2)
    small_len = 2 * feats + span + feats * experts
    small_rows = -(-small_len // cols)
    small = pad_to(
        jnp.concatenate([attn_gain, ffn_gain, segments[0].astype(BF), router_weight.reshape(-1)]),
        small_rows * cols,
    ).reshape(small_rows, cols)
    packed = jnp.concatenate([dense, jnp.broadcast_to(small, (seqs, small_rows, cols))], axis=1)
    packed = jnp.broadcast_to(packed, (rows, seqs, feats + small_rows, cols))
    packed = lax.all_to_all(
        packed.reshape(rows * seqs, feats + small_rows, cols), ALL, 0, 0, tiled=True
    )
    proj = packed[:, :feats].reshape(width, cols)
    small = packed[:, feats:].reshape(rows * seqs, -1)
    gain_one = small[:, :feats].reshape(width).astype(F32)
    gain_two = small[:, feats : 2 * feats].reshape(width).astype(F32)
    segs_all = small[:, 2 * feats : 2 * feats + span].reshape(rows, length)
    row_segs = lax.dynamic_index_in_dim(segs_all, lax.axis_index("row"), 0, False).astype(jnp.int32)
    router_full = small[:, 2 * feats + span : small_len].reshape(width, experts)

    out_full = lax.all_gather(out_weight.T, ALL, axis=0, tiled=True)
    upstream_team = lax.all_gather(cotangent[0], TEAM, axis=0, tiled=True)

    stacked = jnp.stack([gate_weight, up_weight, down_weight.transpose(0, 2, 1)])
    stacked = stacked.reshape(3, near, mine, slab, hidden).transpose(1, 0, 2, 3, 4)
    stacked = jnp.broadcast_to(stacked, (far, near, 3, mine, slab, hidden))
    stacked = lax.all_to_all(
        stacked.reshape(depth, 3, mine, slab, hidden), DEPTH, 0, 0, tiled=True
    )
    stacked = lax.all_gather(stacked, "core", axis=0, tiled=False)
    stacked = stacked.transpose(2, 3, 1, 0, 4, 5).reshape(3, mine, width, hidden)

    index = jnp.arange(length, dtype=jnp.int32)
    below_one = jnp.sum((row_segs < 1).astype(jnp.int32))
    below_two = jnp.sum((row_segs < 2).astype(jnp.int32))
    starts = jnp.where(row_segs == 0, 0, jnp.where(row_segs == 1, below_one, below_two))
    positions = (index - starts).astype(F32)
    frequency = THETA ** (-jnp.arange(HEAD_DIM // 2, dtype=F32) * 2.0 / HEAD_DIM)
    angles = positions[:, None] * frequency
    cosines, sines = jnp.cos(angles), jnp.sin(angles)
    row_f = row_hidden.astype(F32)
    row_inv = lax.rsqrt(jnp.mean(row_f * row_f, axis=-1, keepdims=True) + EPS)
    attn_in = (row_f * row_inv * gain_one).astype(BF)
    pre = nn(attn_in, proj)
    query_rot = rotate(pre[:, :query_cols], cosines, sines).astype(BF)
    key_rot = rotate(pre[:, query_cols : query_cols + key_cols], cosines, sines).astype(BF)
    value_low = pre[:, query_cols + key_cols :].astype(BF)
    allowed = (index[None, :] <= index[:, None]) & (row_segs[:, None] == row_segs[None, :])

    def head(array, number):
        return array[:, number * HEAD_DIM : (number + 1) * HEAD_DIM]

    kept, mixes = [], []
    for number in range(heads):
        kv = number // groups
        scores = nt(head(query_rot, number), head(key_rot, kv)) * scale
        scores = jnp.where(allowed, scores, NEG)
        top = jnp.max(scores, axis=-1, keepdims=True)
        raised = jnp.exp(scores - top)
        probs = raised / jnp.sum(raised, axis=-1, keepdims=True)
        kept.append(probs)
        mixes.append(nn(probs.astype(BF), head(value_low, kv)))
    mix_full = jnp.concatenate(mixes, axis=1)
    mix_low = lax.all_to_all(
        mix_full.astype(BF).reshape(seqs, span, query_cols), SEQ, 0, 0, tiled=True
    )
    mix_low = mix_low.transpose(1, 0, 2).reshape(span, width)

    own_f = own.astype(F32)
    residual = own_f + nt(mix_low, out_full)
    inv_two = lax.rsqrt(jnp.mean(residual * residual, axis=-1, keepdims=True) + EPS)
    ffn_in = (residual * inv_two * gain_two).astype(BF)
    logits = nn(ffn_in, router_full)
    named = jnp.any(routes[0][:, :, None] == jnp.arange(experts, dtype=jnp.int32), axis=1)
    logits = jnp.where(named, logits, NEG)
    raised = jnp.where(named, jnp.exp(logits - jnp.max(logits, axis=-1, keepdims=True)), 0.0)
    gates = raised / jnp.sum(raised, axis=-1, keepdims=True)
    gates_high = gates.astype(BF)
    gates_rest = (gates - gates_high.astype(F32)).astype(BF)
    extra = jnp.concatenate(
        [gates_high, gates_rest, jnp.zeros((span, 128 - 2 * experts), BF)], axis=1
    )
    team = lax.all_gather(jnp.concatenate([ffn_in, extra], axis=1), TEAM, axis=0, tiled=True)

    team_in = team[:, :width]
    team_up = upstream_team.astype(F32)
    first_expert = lax.axis_index("row") * held + lax.axis_index("zl") * mine
    grads = []
    out_sum, slope_sum, slope_cols = 0.0, 0.0, 0.0
    for number in range(mine):
        lane = (jnp.arange(experts) == first_expert + number).astype(F32)
        gate = jnp.sum(
            (
                team[:, width : width + experts].astype(F32)
                + team[:, width + experts : width + 2 * experts].astype(F32)
            )
            * lane,
            axis=1,
            keepdims=True,
        )
        gate_w, up_w, down_w = stacked[0, number], stacked[1, number], stacked[2, number]
        gate_pre = nn(team_in, gate_w)
        up_pre = nn(team_in, up_w)
        sigmoid = jax.nn.sigmoid(gate_pre)
        act = (gate_pre * sigmoid * up_pre).astype(BF)
        expert_out = nt(act, down_w)
        routed_slope = (gate * team_up).astype(BF)
        gate_slope = jnp.sum(team_up * expert_out, axis=1, keepdims=True)
        out_sum = out_sum + gate * expert_out
        hidden_slope = nn(routed_slope, down_w)
        down_grad = tn(routed_slope, act)
        gate_low = (hidden_slope * up_pre * sigmoid * (1.0 + gate_pre * (1.0 - sigmoid))).astype(BF)
        up_low = (hidden_slope * gate_pre * sigmoid).astype(BF)
        gate_grad = tn(team_in, gate_low)
        up_grad = tn(team_in, up_low)
        slope_sum = slope_sum + nt(gate_low, gate_w) + nt(up_low, up_w)
        slope_cols = slope_cols + gate_slope * lane
        grads.append(jnp.stack([gate_grad, up_grad, down_grad]))
    slope_send = jnp.concatenate(
        [
            slope_sum.astype(BF),
            slope_cols.astype(BF),
            jnp.zeros((slope_sum.shape[0], 128 - experts), BF),
        ],
        axis=1,
    )

    def to_owners(partial):
        wide = partial.shape[1]
        step = lax.all_to_all(
            partial.reshape(rows, near * span, wide), "row", 0, 0, tiled=True
        )
        step = jnp.sum(step.astype(F32), axis=0).astype(BF)
        step = lax.all_to_all(step.reshape(near, span, wide), "zl", 0, 0, tiled=True)
        return jnp.sum(step.astype(F32), axis=0)

    slope_back = to_owners(slope_send)
    hidden_out = (residual + to_owners(out_sum.astype(BF))).astype(BF)

    grads = jnp.stack(grads, axis=1).astype(BF)
    grads = grads.reshape(3, mine, depth, cores, slab, hidden).transpose(3, 2, 0, 1, 4, 5)
    grads = lax.all_to_all(grads, "core", 0, 0, tiled=True)
    grads = jnp.sum(grads.astype(F32), axis=0).astype(BF)
    grads = lax.all_to_all(grads, DEPTH, 0, 0, tiled=True)
    grads = grads.reshape(far, near, 3, mine, slab, hidden).astype(F32).sum(axis=0)
    grads = grads.transpose(1, 0, 2, 3, 4).reshape(3, held, slab, hidden)

    token_slope = slope_back[:, :width]
    gate_slope = slope_back[:, width : width + experts]
    logit_slope = (
        gates * (gate_slope - jnp.sum(gates * gate_slope, axis=-1, keepdims=True))
    ).astype(BF)
    router_part = tn(ffn_in, logit_slope)
    ffn_slope = token_slope + nt(logit_slope, router_full)
    upstream = cotangent[0].astype(F32)
    scaled_two = ffn_slope * gain_two
    ffn_gain_part = jnp.sum(ffn_slope * residual * inv_two, axis=0)
    resid_slope = (
        upstream
        + inv_two * scaled_two
        - residual * inv_two**3 * jnp.mean(scaled_two * residual, axis=-1, keepdims=True)
    )
    branch_low = resid_slope.astype(BF)
    out_part = tn(branch_low, mix_low).astype(BF)
    out_part = lax.psum_scatter(out_part, "row", scatter_dimension=0, tiled=True)
    out_grad = lax.psum_scatter(out_part, SEQ, scatter_dimension=0, tiled=True)
    mix_slope = nn(branch_low, out_full).astype(BF)
    mix_slope = mix_slope.reshape(span, seqs, query_cols).transpose(1, 0, 2)
    mix_slope = lax.all_to_all(mix_slope, SEQ, 0, 0, tiled=True).reshape(length, query_cols)

    query_acc, key_acc, value_acc = [], [0.0] * key_heads, [0.0] * key_heads
    for number in range(heads):
        kv = number // groups
        probs, slope = kept[number], head(mix_slope, number)
        delta = jnp.sum(slope.astype(F32) * mixes[number], axis=-1, keepdims=True)
        prob_slope = nt(slope, head(value_low, kv))
        score_low = (probs * (prob_slope - delta)).astype(BF)
        value_acc[kv] = value_acc[kv] + tn(probs.astype(BF), slope)
        query_acc.append(nn(score_low, head(key_rot, kv)) * scale)
        key_acc[kv] = key_acc[kv] + tn(score_low, head(query_rot, number)) * scale
    lows = jnp.concatenate(
        [
            rotate(jnp.concatenate(query_acc, axis=1), cosines, -sines),
            rotate(jnp.concatenate(key_acc, axis=1), cosines, -sines),
            jnp.concatenate(value_acc, axis=1),
        ],
        axis=1,
    ).astype(BF)
    proj_part = tn(attn_in, lows)
    attn_gain_part = jnp.sum(proj_part * proj.astype(F32), axis=1) / gain_one
    attn_slope = nt(lows, proj).astype(BF)
    attn_slope = lax.psum_scatter(attn_slope, SEQ, scatter_dimension=0, tiled=True).astype(F32)

    blocks = rows * seqs
    send_small = jnp.concatenate(
        [
            attn_gain_part.reshape(blocks, feats),
            ffn_gain_part.reshape(blocks, feats),
            router_part.reshape(blocks, feats * experts),
        ],
        axis=1,
    )
    back_len = send_small.shape[1]
    back_rows = -(-back_len // cols)
    send_small = jnp.concatenate(
        [send_small, jnp.zeros((blocks, back_rows * cols - back_len), F32)], axis=1
    ).reshape(blocks, back_rows, cols)
    send = jnp.concatenate([proj_part.reshape(blocks, feats, cols), send_small], axis=1).astype(BF)
    back = lax.all_to_all(send, ALL, 0, 0, tiled=True).astype(F32)
    small_back = jnp.sum(back[:, feats:], axis=0).reshape(-1)
    attn_gain_grad = small_back[:feats]
    ffn_gain_grad = small_back[feats : 2 * feats]
    router_grad = small_back[2 * feats : back_len].reshape(feats, experts)
    proj_back = jnp.sum(back[:, :feats].reshape(rows, seqs, feats, cols), axis=0)
    query_grad = proj_back[:, :, :query_cols].transpose(1, 0, 2).reshape(feats, HEADS * HEAD_DIM)

    def key_grads(part):
        share = seqs * key_heads // KV_HEADS
        part = part.reshape(seqs // share, share, feats, key_cols).sum(axis=1)
        return part.transpose(1, 0, 2).reshape(feats, KV_HEADS * HEAD_DIM)

    key_grad = key_grads(proj_back[:, :, query_cols : query_cols + key_cols])
    value_grad = key_grads(proj_back[:, :, query_cols + key_cols :])

    inv_one = lax.rsqrt(jnp.mean(own_f * own_f, axis=-1, keepdims=True) + EPS)
    scaled_one = attn_slope * gain_one
    hidden_grad = (
        resid_slope
        + inv_one * scaled_one
        - own_f * inv_one**3 * jnp.mean(scaled_one * own_f, axis=-1, keepdims=True)
    ).astype(BF)
    return (
        hidden_out[None],
        hidden_grad[None],
        attn_gain_grad,
        query_grad,
        key_grad,
        value_grad,
        out_grad.astype(F32).T,
        ffn_gain_grad,
        router_grad,
        grads[0],
        grads[1],
        grads[2].transpose(0, 2, 1),
    )


def solution(mesh):
    rows, seqs = mesh.shape["row"], mesh.shape["seq"]
    depth = seqs // 2
    held = 16 // rows
    near = min(GROUP, held, depth)
    fine = Mesh(mesh.devices.reshape(rows, depth // near, near, 2), ALL)
    token = P("row", SEQ, None)
    return jax.shard_map(
        shards,
        mesh=fine,
        in_specs=(
            token,
            P("row", SEQ),
            token,
            token,
            P(ALL),
            P(ALL, None),
            P(ALL, None),
            P(ALL, None),
            P(None, ALL),
            P(ALL),
            P(ALL, None),
            token,
            token,
            P("row", None, SEQ),
        ),
        out_specs=(
            token,
            token,
            P(ALL),
            P(ALL, None),
            P(ALL, None),
            P(ALL, None),
            P(None, ALL),
            P(ALL),
            P(ALL, None),
            token,
            token,
            P("row", None, SEQ),
        ),
        check_vma=False,
    )
```

time: 1580 us -> 674 us (0.43)
  waiting for transfers between devices: 1080 us -> 427 us
  blocking collectives: 201 us -> 6.26 us
  local copies, waits for them, and re-layouts: 123 us -> 51.5 us
  starting transfers between devices: 8.75 us -> 44.6 us
  matrix products: 97.2 us -> 75.2 us
    reduce_scatter x6 -> x2, waiting for transfers between devices: 652 us -> 25.5 us  [the longest x1 25.5 us: shards(): out_grad = lax.psum_scatter(out_part, SEQ, scatter_dimension=0, tiled=True)]
    all_to_all x2 -> x10, waiting for transfers between devices: 25.8 us -> 231 us  [the longest x2 81 us: to_owners(): lax.all_to_all(partial.reshape(rows, near * span, wide), 'row', 0, 0, til...]
    unnamed x23 -> x9, waiting for transfers between devices: 152 us -> 1.53 us
    unnamed x2 -> x0, blocking collectives: 80.8 us -> none
    all_gather x9 -> x5, waiting for transfers between devices: 249 us -> 169 us  [the longest x1 94.1 us: shards(): lax.all_gather(jnp.concatenate([ffn_in, extra], axis=1), TEAM, axis=0, ti...]
    all_to_all x2 -> x1, blocking collectives: 69.3 us -> 6.26 us  [shards(): grads = lax.all_to_all(grads, 'core', 0, 0, tiled=True)]
    gather x13 -> x0, local copies, waits for them, and re-layouts: 53.4 us -> none  [the longest x5 38.8 us: single(): return jnp.take(rows_here, pick_rows, axis=0)]
    all_gather x2 -> x0, blocking collectives: 51.4 us -> none  [the longest x1 40.6 us: shards(): lax.all_gather(router_weight, ('row', 'seq'), axis=0, tiled=True)]
  transfers between devices with their start and end apart: 21 -> 18, of which waited for: 18 -> 15; matrix products, arithmetic and copies ran while one was open for 10% -> 22% of each run, Pallas kernels for 0% -> 0%
where the time goes in v1:
time: 674 us; the launch traced here: 664 us
  waiting for transfers between devices  427 us (63%)
  matrix products  75.2 us (11%)
  local copies, waits for them, and re-layouts  51.5 us (8%)
  starting transfers between devices  44.6 us (7%)
  other arithmetic  43 us (6%)
  between operations  16 us (2%)
    all_gather x1, waiting for transfers between devices, shards(): lax.all_gather(jnp.concatenate([ffn_in, extra], axis=1), TEAM, axis=0, ti...  94.1 us
    all_to_all x2, waiting for transfers between devices, to_owners(): lax.all_to_all(partial.reshape(rows, near * span, wide), 'row', 0, 0, til...  81 us
    all_gather x1, waiting for transfers between devices, shards(): upstream_team = lax.all_gather(cotangent[0], TEAM, axis=0, tiled=True)  64.1 us
    all_to_all x1, waiting for transfers between devices, shards(): grads = lax.all_to_all(grads, DEPTH, 0, 0, tiled=True)  43.3 us
    all_to_all x1, waiting for transfers between devices, shards(): lax.all_to_all(stacked.reshape(depth, 3, mine, slab, hidden), DEPTH, 0, 0...  34.5 us
    all_to_all x2, waiting for transfers between devices, to_owners(): lax.all_to_all(step.reshape(near, span, wide), 'zl', 0, 0, tiled=True)  31.1 us
    dot_general x10, matrix products, nn(): lax.dot_general(left, right, (((1,), (0,)), ((), ())), preferred_element_...  26.2 us
    reduce_scatter x1, waiting for transfers between devices, shards(): out_grad = lax.psum_scatter(out_part, SEQ, scatter_dimension=0, tiled=True)  25.5 us
  transfers between devices with their start and end apart: 18, of which 15 were waited for; matrix products, arithmetic and copies ran while one was open for 22% of the time, Pallas kernels for 0%

profile of v1, /device:TPU:0, one launch (start us, length us, event | category | flops | bytes accessed | tf_op | source)
XLA Modules:
  0.0 663.6 jit_solution(3875653554774515468)
XLA Ops:
  25.5 7.3 %all-to-all-start = ((bf16[32,35,256]{2,1,0:T(8,128)(2,1)}), bf16[32,35,256]{2,1,0:T(8,128)(2,1)S(1)}, u32[]{:S(2)}, u32[]{:S(2)}) async-start(bf16[32,35,256]{2,1,0:T(8,128)(2,1)} %bitcast.19), calls=%async_computation | async-start | bytes 1310720 | tf_op jit(solution)/shard_map/all_to_all | solution.py:101
  34.4 21.8 %all-to-all-done = bf16[32,35,256]{2,1,0:T(8,128)(2,1)S(1)} async-done(((bf16[32,35,256]{2,1,0:T(8,128)(2,1)}), bf16[32,35,256]{2,1,0:T(8,128)(2,1)S(1)}, u32[]{:S(2)}, u32[]{:S(2)}) %all-to-all-start) | async-done | bytes 573472 | tf_op jit(solution)/shard_map/all_to_all | solution.py:101
  64.1 34.5 %all-to-all-done.2 = bf16[4,3,1,128,512]{4,3,1,2,0:T(8,128)(2,1)S(1)} async-done(((bf16[4,3,1,128,512]{4,3,1,2,0:T(8,128)(2,1)}), bf16[4,3,1,128,512]{4,3,1,2,0:T(8,128)(2,1)S(1)}, u32[]{:S(2)}, u32[]{:S(2)}) %all-to-all-start.2) | async-done | bytes 1572896 | tf_op jit(solution)/shard_map/all_to_all | solution.py:118
  119.0 6.2 all-gather.9.cloned.1.call-done
  144.0 94.1 %all-gather.11.cloned.1.call-done = bf16[2048,1152]{0,1:T(8,128)(2,1)} async-done(((bf16[128,1152]{0,1:T(8,128)(2,1)}), bf16[2048,1152]{0,1:T(8,128)(2,1)}) %all-gather.11.cloned.1.call-update) | async-done | bytes 4718608 | tf_op jit(solution)/shard_map/all_gather | solution.py:174
  239.1 7.1 %fusion.14 = f32[2048,512]{1,0:T(8,128)} fusion(bf16[1024,512]{1,0:T(8,128)(2,1)} %bitcast.219, bf16[2048,1152]{0,1:T(8,128)(2,1)} %all-gather.11.cloned.1.call-done), kind=kOutput, calls=%fused_computation.36 | convolution fusion | flops 2147483648 | bytes 9437184 | tf_op jit(solution)/shard_map/dot_general | solution.py:30
  246.2 4.5 fusion.16
  250.7 64.1 %all-gather.17.cloned.1.call-done = bf16[1,2048,1024]{2,1,0:T(8,128)(2,1)} async-done(((bf16[1,128,1024]{2,1,0:T(8,128)(2,1)}), bf16[1,2048,1024]{2,1,0:T(8,128)(2,1)}) %all-gather.17.cloned.1.call-update) | async-done | bytes 4194320 | tf_op jit(solution)/shard_map/all_gather | solution.py:113
  314.8 9.5 %multiply_convert_fusion.3 = (bf16[2048,512]{1,0:T(8,128)(2,1)}, bf16[2048,512]{1,0:T(8,128)(2,1)}, bf16[2048,512]{1,0:T(8,128)(2,1)S(1)}) fusion(f32[2048,512]{1,0:T(8,128)} %fusion.16, f32[2048,512]{1,0:T(8,128)} %fusion.14, bf16[1024,512]{1,0:T(8,128)(2,1)} %bitcast.223, bf16[1,2048,1024]{2,1,0:T(8,128)(2,1)} %all-gather.17.cloned.1.call-done, ...), kind=kOutput, calls=%fused_computation.15 | convolution fusion | flops 2170552320 | bytes 19931136 | tf_op jit(solution)/shard_map/dot_general | solution.py:30
  328.7 5.0 all-to-all-start.3
  347.3 32.8 %all-to-all-done.3 = bf16[4,512,1024]{2,1,0:T(8,128)(2,1)} async-done(((bf16[4,512,1024]{2,1,0:T(8,128)(2,1)}), bf16[4,512,1024]{2,1,0:T(8,128)(2,1)}, u32[]{:S(2)}, u32[]{:S(2)}) %all-to-all-start.3) | async-done | bytes 4194336 | tf_op jit(solution)/shard_map/all_to_all | solution.py:221
  380.2 5.0 all-to-all-start.5
  389.5 48.1 %all-to-all-done.5 = bf16[4,512,1152]{1,2,0:T(8,128)(2,1)} async-done(((bf16[4,512,1152]{1,2,0:T(8,128)(2,1)}), bf16[4,512,1152]{1,2,0:T(8,128)(2,1)}, u32[]{:S(2)}, u32[]{:S(2)}) %all-to-all-start.5) | async-done | bytes 4718624 | tf_op jit(solution)/shard_map/all_to_all | solution.py:221
  437.7 4.4 all-to-all-start.4
  442.1 4.5 reduce_sum.252
  449.1 18.1 %all-to-all-done.4 = bf16[4,128,1024]{2,1,0:T(8,128)(2,1)} async-done(((bf16[4,128,1024]{2,1,0:T(8,128)(2,1)}), bf16[4,128,1024]{2,1,0:T(8,128)(2,1)}, u32[]{:S(2)}, u32[]{:S(2)}) %all-to-all-start.4) | async-done | bytes 1048608 | tf_op jit(solution)/shard_map/all_to_all | solution.py:225
  467.1 4.5 all-to-all-start.6
  472.5 6.3 fusion.25
  486.6 13.1 %all-to-all-done.6 = bf16[4,128,1152]{1,2,0:T(8,128)(2,1)} async-done(((bf16[4,128,1152]{1,2,0:T(8,128)(2,1)}), bf16[4,128,1152]{1,2,0:T(8,128)(2,1)}, u32[]{:S(2)}, u32[]{:S(2)}) %all-to-all-start.6) | async-done | bytes 1179680 | tf_op jit(solution)/shard_map/all_to_all | solution.py:225
  509.9 6.2 fusion.28
  534.8 6.3 all_to_all.55
  556.3 43.3 %all-to-all-done.10 = bf16[4,3,1,128,512]{4,3,2,1,0:T(8,128)(2,1)S(1)} async-done(((bf16[4,3,1,128,512]{4,3,2,1,0:T(8,128)(2,1)}), bf16[4,3,1,128,512]{4,3,2,1,0:T(8,128)(2,1)S(1)}, u32[]{:S(2)}, u32[]{:S(2)}) %all-to-all-start.10) | async-done | bytes 1572896 | tf_op jit(solution)/shard_map/all_to_all | solution.py:235
  606.6 16.1 %all-to-all-done.8 = bf16[32,35,256]{2,1,0:T(8,128)(2,1)S(1)} async-done(((bf16[32,35,256]{2,1,0:T(8,128)(2,1)}), bf16[32,35,256]{2,1,0:T(8,128)(2,1)S(1)}, u32[]{:S(2)}, u32[]{:S(2)}) %all-to-all-start.8) | async-done | bytes 573472 | tf_op jit(solution)/shard_map/all_to_all | solution.py:300
  629.2 25.5 %reduce-scatter.8.cloned.1.call-done = bf16[32,1024]{1,0:T(8,128)(2,1)} async-done(((bf16[256,1024]{1,0:T(8,128)(2,1)}), bf16[32,1024]{1,0:T(8,128)(2,1)}) %reduce-scatter.8.cloned.1.call-update) | async-done | bytes 65552 | tf_op jit(solution)/shard_map/reduce_scatter | solution.py:257
  (353 shorter events, 159.2 us)
Async XLA Ops:
  7.2 92.5 %all-gather.13.cloned.1.call-start = ((), (), s32[]{:S(2)}) async-start(), calls=%async_computation.18 | async-start | bytes 2359296 | tf_op jit(solution)/shard_map/all_gather | solution.py:84
  7.9 117.3 %all-gather.9.cloned.1.call-start = ((), (), s32[]{:S(2)}) async-start(), calls=%async_computation.14 | async-start | bytes 2162688 | tf_op jit(solution)/shard_map/all_gather | solution.py:112
  25.5 30.7 %all-to-all-start = ((bf16[32,35,256]{2,1,0:T(8,128)(2,1)}), bf16[32,35,256]{2,1,0:T(8,128)(2,1)S(1)}, u32[]{:S(2)}, u32[]{:S(2)}) async-start(bf16[32,35,256]{2,1,0:T(8,128)(2,1)} %bitcast.19), calls=%async_computation | async-start | bytes 1310720 | tf_op jit(solution)/shard_map/all_to_all | solution.py:101
  56.2 42.3 %all-to-all-start.2 = ((bf16[4,3,1,128,512]{4,3,1,2,0:T(8,128)(2,1)}), bf16[4,3,1,128,512]{4,3,1,2,0:T(8,128)(2,1)S(1)}, u32[]{:S(2)}, u32[]{:S(2)}) async-start(bf16[4,3,1,128,512]{4,3,1,2,0:T(8,128)(2,1)} %maximum_bitcast_fusion), calls=%async_computation.2 | async-start | bytes 3145728 | tf_op jit(solution)/shard_map/all_to_all | solution.py:118
  59.8 79.0 %all-gather.15.cloned.1.call-start = ((), (), s32[]{:S(2)}) async-start(), calls=%async_computation.19 | async-start | bytes 4718592 | tf_op jit(solution)/shard_map/all_gather | solution.py:121
  59.9 44.6 %copy-start.68 = (f32[32]{0:T(128)}, f32[32]{0:T(128)S(1)}, u32[]{:S(2)}) copy-start(f32[32]{0:T(128)S(1)} %multiply_power_fusion) | copy-start | bytes 388
  60.8 43.6 %copy-start.47 = (f32[1024]{0:T(1024)}, f32[1024]{0:T(1024)S(1)}, u32[]{:S(2)}) copy-start(f32[1024]{0:T(1024)S(1)} %reshape.568) | copy-start | bytes 12292
  60.8 46.4 %copy-start.17 = (bf16[32,32,256]{2,1,0:T(8,128)(2,1)}, bf16[32,32,256]{2,1,0:T(8,128)(2,1)S(1)}, u32[]{:S(2)}) copy-start(bf16[32,32,256]{2,1,0:T(8,128)(2,1)S(1)} %slice.239) | copy-start | bytes 1572868
  64.0 43.2 %copy-start.21 = (f32[1024,32]{0,1:T(8,128)}, f32[1024,32]{0,1:T(8,128)S(1)}, u32[]{:S(2)}) copy-start(f32[1024,32]{0,1:T(8,128)S(1)} %get-tuple-element.147) | copy-start | bytes 393220
  114.2 13.5 %all-to-all-start.1 = ((bf16[8,128,128]{1,2,0:T(8,128)(2,1)}), bf16[8,128,128]{1,2,0:T(8,128)(2,1)S(1)}, u32[]{:S(2)}, u32[]{:S(2)}) async-start(bf16[8,128,128]{1,2,0:T(8,128)(2,1)} %pad_maximum_fusion.5), calls=%async_computation.1 | async-start | bytes 524288 | tf_op jit(solution)/shard_map/all_to_all | solution.py:155
  117.6 120.5 %all-gather.11.cloned.1.call-start = ((), (), s32[]{:S(2)}) async-start(), calls=%async_computation.15 | async-start | bytes 5013504 | tf_op jit(solution)/shard_map/all_gather | solution.py:174
  133.7 181.2 %all-gather.17.cloned.1.call-start = ((), (), s32[]{:S(2)}) async-start(), calls=%async_computation.20 | async-start | bytes 4456448 | tf_op jit(solution)/shard_map/all_gather | solution.py:113
  140.8 97.3 %copy-start.76 = (f32[16]{0:T(128)S(1)}, f32[16]{0:T(128)}, u32[]{:S(2)}) copy-start(f32[16]{0:T(128)} %compare_convert_fusion) | copy-start | bytes 196
  239.1 85.2 %copy-start.64 = (f32[2048]{0:T(1024)}, f32[2048]{0:T(1024)S(1)}, u32[]{:S(2)}) copy-start(f32[2048]{0:T(1024)S(1)} %multiply_reduce_fusion.6) | copy-start | bytes 24580
  328.7 51.5 %all-to-all-start.3 = ((bf16[4,512,1024]{2,1,0:T(8,128)(2,1)}), bf16[4,512,1024]{2,1,0:T(8,128)(2,1)}, u32[]{:S(2)}, u32[]{:S(2)}) async-start(bf16[4,512,1024]{2,1,0:T(8,128)(2,1)} %bitcast.202), calls=%async_computation.3 | async-start | bytes 8388608 | tf_op jit(solution)/shard_map/all_to_all | solution.py:221
  380.2 57.5 %all-to-all-start.5 = ((bf16[4,512,1152]{1,2,0:T(8,128)(2,1)}), bf16[4,512,1152]{1,2,0:T(8,128)(2,1)}, u32[]{:S(2)}, u32[]{:S(2)}) async-start(bf16[4,512,1152]{1,2,0:T(8,128)(2,1)} %bitcast.198), calls=%async_computation.5 | async-start | bytes 9437184 | tf_op jit(solution)/shard_map/all_to_all | solution.py:221
  437.7 29.5 %all-to-all-start.4 = ((bf16[4,128,1024]{2,1,0:T(8,128)(2,1)}), bf16[4,128,1024]{2,1,0:T(8,128)(2,1)}, u32[]{:S(2)}, u32[]{:S(2)}) async-start(bf16[4,128,1024]{2,1,0:T(8,128)(2,1)} %bitcast.204), calls=%async_computation.4 | async-start | bytes 2097152 | tf_op jit(solution)/shard_map/all_to_all | solution.py:225
  467.1 32.6 %all-to-all-start.6 = ((bf16[4,128,1152]{1,2,0:T(8,128)(2,1)}), bf16[4,128,1152]{1,2,0:T(8,128)(2,1)}, u32[]{:S(2)}, u32[]{:S(2)}) async-start(bf16[4,128,1152]{1,2,0:T(8,128)(2,1)} %copy_bitcast_fusion.2), calls=%async_computation.6 | async-start | bytes 2359296 | tf_op jit(solution)/shard_map/all_to_all | solution.py:225
  505.8 13.8 %all-to-all-start.7 = ((bf16[8,128,128]{1,2,0:T(8,128)(2,1)}), bf16[8,128,128]{1,2,0:T(8,128)(2,1)}, u32[]{:S(2)}, u32[]{:S(2)}) async-start(bf16[8,128,128]{1,2,0:T(8,128)(2,1)} %bitcast.53), calls=%async_computation.7 | async-start | bytes 524288 | tf_op jit(solution)/shard_map/all_to_all | solution.py:260
  509.8 116.3 %reduce-scatter.6.cloned.1.call-start = ((), (), s32[]{:S(2)}) async-start(), calls=%async_computation.16 | async-start | bytes 2621440 | tf_op jit(solution)/shard_map/reduce_scatter | solution.py:256
  518.2 108.5 %reduce-scatter.10.cloned.1.call-start = ((), (), s32[]{:S(2)}) async-start(), calls=%async_computation.21 | async-start | bytes 2359296
  546.5 53.2 %all-to-all-start.10 = ((bf16[4,3,1,128,512]{4,3,2,1,0:T(8,128)(2,1)}), bf16[4,3,1,128,512]{4,3,2,1,0:T(8,128)(2,1)S(1)}, u32[]{:S(2)}, u32[]{:S(2)}) async-start(bf16[4,3,1,128,512]{4,3,2,1,0:T(8,128)(2,1)} %copy.271), calls=%async_computation.12 | async-start | bytes 3145728 | tf_op jit(solution)/shard_map/all_to_all | solution.py:235
  599.7 23.0 %all-to-all-start.8 = ((bf16[32,35,256]{2,1,0:T(8,128)(2,1)}), bf16[32,35,256]{2,1,0:T(8,128)(2,1)S(1)}, u32[]{:S(2)}, u32[]{:S(2)}) async-start(bf16[32,35,256]{2,1,0:T(8,128)(2,1)} %pad_maximum_fusion.1), calls=%async_computation.8 | async-start | bytes 1310720 | tf_op jit(solution)/shard_map/all_to_all | solution.py:300
  602.3 52.5 %reduce-scatter.8.cloned.1.call-start = ((), (), s32[]{:S(2)}) async-start(), calls=%async_computation.17 | async-start | bytes 589824 | tf_op jit(solution)/shard_map/reduce_scatter | solution.py:257
  (76 other events, 559.3 us)
Sparse Core Ops, SparseCore 0:
  9.6 36.3 all-gather.12
  49.0 76.1 all-gather.8
  126.8 11.9 all-gather.14
  141.3 96.7 all-gather.10
  240.7 74.0 all-gather.16
  518.4 34.7 reduce-scatter.5
  555.5 52.1 reduce-scatter.9
  626.3 28.4 reduce-scatter.7
